TPU v7x, 768 devices: a whole 4x8x12 slice. The times are simulated.
768 devices in a mesh: expert: 4 (over x), tensor: 16 (over y, core), dp: 12 (over z).
Axes of the slice: x: 4, y: 8, z: 12, core: 2. Of those that a mesh axis runs over, the one named last changes fastest.
Arguments:
- grad_out: bfloat16 [12, 1024, 2048], P('dp', 'expert', 'tensor'), may hold values from -6 to 6
- routes: int32 [12, 1024, 8], P('dp', 'expert'), may hold values from 0 to 63, all different within a row; in each aligned block of 256 rows (0 to 255, 256 to 511, ..., all dimensions but the last counted through in order) at most 64 rows name the same one
- gates: bfloat16 [12, 1024, 8], P('dp', 'expert'), may hold values from 0.019897461 to 0.5
- hidden: bfloat16 [64, 3072, 768], P('expert', 'dp'), may hold values from -6 to 6
- w_down: bfloat16 [64, 768, 2048], P('expert', None, 'tensor'), may hold values from -0.21875 to 0.21875
Outputs:
- grad_hidden: bfloat16 [64, 3072, 768], P('expert', ('dp', 'tensor'))
- grad_weight: bfloat16 [64, 768, 2048], P('expert', 'dp', 'tensor')
- grad_gates: float32 [12, 1024, 8], P('dp', 'expert')
Inputs may be any that keep to these rules, and one draw needn't show every extreme that they name: `routes`: among the 256 tokens of one block, no expert is named by more than 64 pairs; some expert is named by exactly 64. A token names 8 different experts.
All inputs are finite; a program needn't handle non-finite values.
Results may differ from a plain program's by a relative error of at most 0.023.
Values may be sent and summed in bfloat16 or wider, within the bound.
A program may use at most 64 MiB of HBM per device.

v0:
```python
import jax
import jax.numpy as jnp
from jax import lax
from jax.sharding import PartitionSpec as P


def on_device(grad_out, routes, gates, hidden, w_down):
    groups = lax.axis_size("expert")
    local_experts = w_down.shape[0]
    experts = groups * local_experts
    tok_rows = grad_out.shape[1]
    top_k = routes.shape[2]
    width_part = grad_out.shape[2]
    capacity = hidden.shape[1] // groups
    slot_count = groups * capacity
    chosen = routes.reshape(tok_rows * top_k)
    expert_hot = (chosen[:, None] == jnp.arange(experts, dtype=jnp.int32)[None, :]).astype(
        jnp.int32
    )
    earlier = jnp.cumsum(expert_hot, 0) - expert_hot
    rank = jnp.sum(earlier * expert_hot, 1)
    target = chosen * capacity + rank
    pair_token = jnp.arange(tok_rows * top_k, dtype=jnp.int32) // top_k
    token_rows = grad_out[0][pair_token]
    sent_rows = jnp.zeros((experts * capacity, width_part), jnp.bfloat16).at[target].set(token_rows)
    sent_gates = (
        jnp.zeros((experts * capacity,), jnp.bfloat16)
        .at[target]
        .set(gates.reshape(tok_rows * top_k))
    )
    rows_in, gates_in = (
        lax.all_to_all(
            sent_rows.reshape(groups, local_experts, capacity, width_part),
            "expert",
            split_axis=0,
            concat_axis=2,
            tiled=True,
        ),
        lax.all_to_all(
            sent_gates.reshape(groups, local_experts, capacity),
            "expert",
            split_axis=0,
            concat_axis=2,
            tiled=True,
        ),
    )
    rows_in = rows_in.reshape(local_experts, slot_count, width_part)
    gates_in = gates_in.reshape(local_experts, slot_count)
    scaled = (gates_in.astype(jnp.float32)[:, :, None] * rows_in.astype(jnp.float32)).astype(
        jnp.bfloat16
    )
    hidden_term = jnp.einsum("esd,ehd->esh", scaled, w_down, preferred_element_type=jnp.float32)
    grad_hidden = lax.psum_scatter(
        hidden_term.astype(jnp.bfloat16), "tensor", scatter_dimension=1, tiled=True
    )
    weight_part = jnp.einsum("esh,esd->ehd", hidden, scaled, preferred_element_type=jnp.float32)
    grad_weight = lax.psum_scatter(
        weight_part.astype(jnp.bfloat16), "dp", scatter_dimension=1, tiled=True
    )
    output_part = jnp.einsum("esh,ehd->esd", hidden, w_down, preferred_element_type=jnp.float32)
    gate_part = jnp.sum(rows_in.astype(jnp.float32) * output_part, 2)
    gate_total = lax.psum(gate_part, "tensor")
    returned = lax.all_to_all(
        gate_total.reshape(local_experts, groups, capacity),
        "expert",
        split_axis=1,
        concat_axis=0,
        tiled=True,
    )
    grad_gates = returned.reshape(experts * capacity)[target]
    return (grad_hidden, grad_weight, grad_gates.reshape(1, tok_rows, top_k))


def solution(mesh):
    placed = (
        P("dp", "expert", "tensor"),
        P("dp", "expert", None),
        P("dp", "expert", None),
        P("expert", "dp", None),
        P("expert", None, "tensor"),
    )
    return jax.shard_map(
        on_device,
        mesh=mesh,
        in_specs=placed,
        out_specs=(
            P("expert", ("dp", "tensor"), None),
            P("expert", "dp", "tensor"),
            P("dp", "expert", None),
        ),
        check_vma=False,
    )
```

profile of v0, /device:TPU:1, one launch (start us, length us, event | category | flops | bytes accessed | tf_op | source)
XLA Modules:
  0.0 274.5 jit_solution(48197616983397392)
XLA Ops:
  7.2 0.9 broadcast_multiply_fusion
  8.0 0.9 copy.38
  9.2 0.8 copy.42
  10.4 0.8 fusion.6
  11.2 34.5 %reduce-window.6 = s32[64,16,128]{2,1,0:T(8,128)} reduce-window(s32[64,16,128]{2,1,0:T(8,128)} %fusion.6, s32[]{:T(128)} %constant.27.clone.1), window={size=1x1x128 pad=0_0x0_0x127_0}, to_apply=%region_0.0 | reduce-window | flops 16646144 | bytes 1048580 | tf_op jit(solution)/shard_map/reduce-window
  45.7 2.1 slice.12
  47.8 1.5 copy.54
  49.5 1.3 broadcast_add_fusion
  50.7 0.3 fusion.2
  51.0 14.6 %scatter_custom_fusion = bf16[4096]{0:T(1024)(128)(2,1)S(1)} fusion(s32[2048]{0:T(1024)S(1)} %bitcast.66, bf16[2048]{0:T(1024)(128)(2,1)S(1)} %reshape.162, bf16[]{:T(256)} %constant.25.clone.1), kind=kCustom, calls=%fused_computation.30 | custom fusion | bytes 8194 | tf_op jit(solution)/shard_map/scatter | solution.py:29
  65.7 0.7 reshape.182
  66.4 4.8 %all-to-all-start = ((bf16[4,2,512]{2,1,0:T(2,128)(2,1)}), bf16[4,2,512]{2,1,0:T(2,128)(2,1)S(1)}, u32[]{:S(2)}, u32[]{:S(2)}) async-start(bf16[4,2,512]{2,1,0:T(2,128)(2,1)} %reshape.182), calls=%async_computation | async-start | bytes 16384 | tf_op jit(solution)/shard_map/all_to_all | solution.py:39
  71.2 20.7 %scatter_custom_fusion.1 = bf16[4096,128]{1,0:T(8,128)(2,1)} fusion(s32[2048]{0:T(1024)S(1)} %bitcast.67, bf16[256,128]{1,0:T(8,128)(2,1)} %bitcast.70, s32[2048]{0:T(1024)S(1)} %broadcast_clamp_fusion.1, bf16[]{:T(256)} %constant.25.clone.1), kind=kCustom, calls=%fused_computation.13 | custom fusion | bytes 1049088 | tf_op jit(solution)/shard_map/scatter | solution.py:25
  91.9 4.2 %all-to-all-start.1 = ((bf16[4,16,64,128]{3,2,1,0:T(8,128)(2,1)}), bf16[4,16,64,128]{3,2,1,0:T(8,128)(2,1)}, u32[]{:S(2)}, u32[]{:S(2)}) async-start(bf16[4,16,64,128]{3,2,1,0:T(8,128)(2,1)} %bitcast.60), calls=%async_computation.1 | async-start | bytes 2097152 | tf_op jit(solution)/shard_map/all_to_all | solution.py:32
  96.6 9.4 %all-to-all-done.1 = bf16[4,16,64,128]{3,2,1,0:T(8,128)(2,1)} async-done(((bf16[4,16,64,128]{3,2,1,0:T(8,128)(2,1)}), bf16[4,16,64,128]{3,2,1,0:T(8,128)(2,1)}, u32[]{:S(2)}, u32[]{:S(2)}) %all-to-all-start.1) | async-done | bytes 1048608 | tf_op jit(solution)/shard_map/all_to_all | solution.py:32
  106.0 1.5 convert_bitcast_fusion.1
  107.7 1.3 copy-done.1
  109.0 6.1 %convert_bitcast_fusion = bf16[16,768,128]{1,2,0:T(8,128)(2,1)} fusion(bf16[16,256,768]{2,1,0:T(8,128)(2,1)} %param.8, f32[16,256,128]{2,1,0:T(8,128)S(1)} %bitcast.57, f32[16,256]{1,0:T(8,128)S(1)} %reshape.138), kind=kOutput, calls=%fused_computation.5 | convolution fusion | flops 807927808 | bytes 11550720 | tf_op jit(solution)/shard_map/esh,esd->ehd/dot_general | solution.py:56
  115.0 5.1 %copy.46 = bf16[16,768,128]{2,0,1:T(8,128)(2,1)} copy(bf16[16,768,128]{1,2,0:T(8,128)(2,1)} %convert_bitcast_fusion) | data formatting | bytes 6291456 | tf_op jit(solution)/shard_map/convert_element_type | solution.py:58
  120.3 6.1 %convolution_convert_fusion = bf16[16,256,768]{2,1,0:T(8,128)(2,1)} fusion(bf16[16,768,128]{2,1,0:T(8,128)(2,1)S(1)} %copy-done, f32[16,256,128]{2,1,0:T(8,128)} %bitcast.58, f32[16,256]{1,0:T(8,128)S(1)} %reshape.138), kind=kOutput, calls=%fused_computation.4 | convolution fusion | flops 809500672 | bytes 11550720 | tf_op jit(solution)/shard_map/esd,ehd->esh/dot_general | solution.py:52
  126.4 3.0 %copy.48 = f32[16,256,128]{1,2,0:T(8,128)} copy(f32[16,256,128]{2,1,0:T(8,128)} %bitcast.59) | data formatting | bytes 4194304 | tf_op jit(solution)/shard_map/convert_element_type | solution.py:49
  129.4 5.6 %multiply_reduce_fusion = f32[16,256]{1,0:T(8,128)S(1)} fusion(f32[16,256,128]{1,2,0:T(8,128)} %copy.48, bf16[16,256,768]{2,1,0:T(8,128)(2,1)} %param.8, bf16[16,768,128]{2,1,0:T(8,128)(2,1)S(1)} %copy-done), kind=kOutput, calls=%fused_computation.7 | convolution fusion | flops 806350848 | bytes 11550720 | tf_op jit(solution)/shard_map/esh,ehd->esd/dot_general | solution.py:60
  135.1 54.6 %psum.7 = f32[16,4,64]{2,1,0:T(4,128)S(1)} all-reduce(f32[16,4,64]{2,1,0:T(4,128)S(1)} %reshape.135), channel_id=1, replica_groups=mesh['expert'=4,'tensor'=16,'dp'=12] {'tensor'}, use_global_device_ids=true, to_apply=%region_8.9 | all-reduce | flops 4096 | bytes 32768 | tf_op jit(solution)/shard_map/psum | solution.py:62
  189.7 0.7 reshape.184
  190.4 3.3 %all-to-all-start.2 = ((f32[4,1,1024]{2,1,0:T(1,128)}), f32[4,1,1024]{2,1,0:T(1,128)S(1)}, u32[]{:S(2)}, u32[]{:S(2)}) async-start(f32[4,1,1024]{2,1,0:T(1,128)} %reshape.184), calls=%async_computation.4 | async-start | bytes 32768 | tf_op jit(solution)/shard_map/all_to_all | solution.py:63
  193.7 4.2 %all-to-all-done.2 = f32[4,1,1024]{2,1,0:T(1,128)S(1)} async-done(((f32[4,1,1024]{2,1,0:T(1,128)}), f32[4,1,1024]{2,1,0:T(1,128)S(1)}, u32[]{:S(2)}, u32[]{:S(2)}) %all-to-all-start.2) | async-done | bytes 16416 | tf_op jit(solution)/shard_map/all_to_all | solution.py:63
  197.8 0.5 broadcast.118
  198.4 0.7 reduce
  199.2 11.8 %gather_fusion = f32[2048]{0:T(1024)S(1)} fusion(f32[4096]{0:T(1024)S(1)} %reshape.136, s32[2048]{0:T(1024)S(1)} %broadcast_clamp_fusion), kind=kCustom, calls=%fused_computation.1 | custom fusion | bytes 24576 | tf_op jit(solution)/shard_map/gather | solution.py:70
  211.1 0.7 copy.51
  211.8 1.7 copy.50
  213.5 54.2 %reduce-scatter.3.cloned.1.call-done = bf16[16,16,768]{2,1,0:T(8,128)(2,1)} async-done(((bf16[16,256,768]{2,1,0:T(8,128)(2,1)}), bf16[16,16,768]{2,1,0:T(8,128)(2,1)}) %reduce-scatter.3.cloned.1.call-update) | async-done | bytes 393232 | tf_op jit(solution)/shard_map/reduce_scatter | solution.py:53
  (31 shorter events, 1.9 us)
Async XLA Ops:
  7.2 113.1 %copy-start = (bf16[16,768,128]{2,1,0:T(8,128)(2,1)S(1)}, bf16[16,768,128]{2,1,0:T(8,128)(2,1)}, u32[]{:S(2)}) copy-start(bf16[16,768,128]{2,1,0:T(8,128)(2,1)} %param.9) | copy-start | bytes 9437188
  66.4 25.6 %all-to-all-start = ((bf16[4,2,512]{2,1,0:T(2,128)(2,1)}), bf16[4,2,512]{2,1,0:T(2,128)(2,1)S(1)}, u32[]{:S(2)}, u32[]{:S(2)}) async-start(bf16[4,2,512]{2,1,0:T(2,128)(2,1)} %reshape.182), calls=%async_computation | async-start | bytes 16384 | tf_op jit(solution)/shard_map/all_to_all | solution.py:39
  91.9 14.1 %all-to-all-start.1 = ((bf16[4,16,64,128]{3,2,1,0:T(8,128)(2,1)}), bf16[4,16,64,128]{3,2,1,0:T(8,128)(2,1)}, u32[]{:S(2)}, u32[]{:S(2)}) async-start(bf16[4,16,64,128]{3,2,1,0:T(8,128)(2,1)} %bitcast.60), calls=%async_computation.1 | async-start | bytes 2097152 | tf_op jit(solution)/shard_map/all_to_all | solution.py:32
  96.2 115.6 %reduce-scatter.5.cloned.1.call-start = ((), (), s32[]{:S(2)}) async-start(), calls=%async_computation.6 | async-start | bytes 3407872 | tf_op jit(solution)/shard_map/reduce_scatter | solution.py:57
  107.7 1.3 copy-start.1
  120.2 147.5 %reduce-scatter.3.cloned.1.call-start = ((), (), s32[]{:S(2)}) async-start(), calls=%async_computation.5 | async-start | bytes 6684672 | tf_op jit(solution)/shard_map/reduce_scatter | solution.py:53
  190.4 7.4 %all-to-all-start.2 = ((f32[4,1,1024]{2,1,0:T(1,128)}), f32[4,1,1024]{2,1,0:T(1,128)S(1)}, u32[]{:S(2)}, u32[]{:S(2)}) async-start(f32[4,1,1024]{2,1,0:T(1,128)} %reshape.184), calls=%async_computation.4 | async-start | bytes 32768 | tf_op jit(solution)/shard_map/all_to_all | solution.py:63
Sparse Core Ops, SparseCore 0:
  120.3 68.2 reduce-scatter.4
  192.3 75.3 reduce-scatter.2
where the time goes:
time: 279 us; the launch traced here: 275 us
  waiting for transfers between devices  67.8 us (24%)
  local copies, waits for them, and re-layouts  67.4 us (24%)
  blocking collectives  54.6 us (20%)
  other arithmetic  40.1 us (14%)
  matrix products  17.8 us (6%)
  between operations  14.2 us (5%)
  starting transfers between devices  12.6 us (5%)
    psum x1, blocking collectives, on_device(): gate_total = lax.psum(gate_part, 'tensor')  54.6 us
    reduce_scatter x1, waiting for transfers between devices, on_device(): lax.psum_scatter(hidden_term.astype(jnp.bfloat16), 'tensor', scatter_dime...  54.2 us
    another operation x3, other arithmetic  36 us
    scatter x1, local copies, waits for them, and re-layouts, on_device(): jnp.zeros((experts * capacity, width_part), jnp.bfloat16).at[target]  20.7 us
    scatter x1, local copies, waits for them, and re-layouts, on_device(): sent_gates = jnp.zeros((experts * capacity,), jnp.bfloat16).at[target].se...  14.6 us
    gather x1, local copies, waits for them, and re-layouts, on_device(): grad_gates = returned.reshape(experts * capacity)[target]  11.8 us
    all_to_all x1, waiting for transfers between devices, on_device(): lax.all_to_all(sent_rows.reshape(groups, local_experts, capacity, width_p...  9.41 us
    unnamed x12, local copies, waits for them, and re-layouts  6.99 us
  transfers between devices with their start and end apart: 5, of which 3 were waited for; matrix products, arithmetic and copies ran while one was open for 19% of the time, Pallas kernels for 0%

commit v1 on v0

v1 whole, which is shorter than its diff:
```python
import functools
import math

import jax
import jax.numpy as jnp
from jax import lax
from jax.experimental import pallas as pl
from jax.experimental.pallas import tpu as pltpu
from jax.sharding import PartitionSpec as P

MESH = pl.DeviceIdType.MESH
BF = jnp.bfloat16
F32 = jnp.float32


def mod(a, n):
    return lax.rem(a, jnp.int32(n))


def div(a, n):
    return lax.div(a, jnp.int32(n))


def kernel(
    nx, ny, nz, groups,
    go_in, routes, gates, hid_in, w_in,
    gh_out, gw_out, gg_out,
    hid, w2, go_all, rg_send, rg, dyh, sc, mh, mg, gcol,
    ty, tz, ry, rz, gall, sgx, gsc,
    hid_sem, wl_sem, ws_sem, wr_sem, go_l, gox_s, gox_r, goc_s, goc_r, rg_s, rg_r,
    ys_sem, yr_sem, zs_sem, zr_sem, ga_s, ga_r, sg_s, sg_r,
):
    top, toks = routes.shape
    width = go_in.shape[1]
    experts, _, _, q, h = hid.shape
    per = experts // groups
    cap = 2 * ny * q // nx
    yb = ny // nx
    half = yb * q
    hz = h // nz
    lanes = ny * q
    x = lax.axis_index("expert")
    t = lax.axis_index("tensor")
    z = lax.axis_index("dp")
    y = div(t, 2)
    c = mod(t, 2)
    peer_c = 1 - c

    def dev(xx, yy, cc, zz):
        return {"expert": xx, "tensor": yy * 2 + cc, "dp": zz}

    def xat(dx):
        return mod(x + dx, nx)

    def yat(dy):
        return mod(y + dy, ny)

    def zat(dz):
        return mod(z + dz, nz)

    peer = dev(x, y, peer_c, z)

    def remote(src, dst, ssem, rsem, to):
        return pltpu.make_async_remote_copy(
            src_ref=src, dst_ref=dst, send_sem=ssem, recv_sem=rsem,
            device_id=to, device_id_type=MESH,
        )

    barrier = pltpu.get_barrier_semaphore()
    partners = [peer]
    partners += [dev(xat(dx), y, mod(c + r, 2), z) for dx in range(1, nx) for r in (0, 1)]
    partners += [dev(x, yat(dy), c, z) for dy in range(1, ny)]
    partners += [dev(x, y, c, zat(dz)) for dz in sorted({1, nz - 1})]
    for partner in partners:
        pl.semaphore_signal(barrier, inc=1, device_id=partner, device_id_type=MESH)

    mine = pl.ds(pl.multiple_of(c * width, width), width)
    others = pl.ds(pl.multiple_of(peer_c * width, width), width)

    def group(g):
        return pl.ds(g * per, per)

    go_local = pltpu.make_async_copy(go_in, go_all.at[x, :, mine], go_l)
    go_local.start()

    def hid_copy(g):
        return pltpu.make_async_copy(hid_in.at[group(g)], hid.at[group(g)], hid_sem.at[g])

    def w_copy(g):
        return pltpu.make_async_copy(w_in.at[group(g)], w2.at[group(g), :, mine], wl_sem.at[g])

    def w_send(g):
        return remote(w_in.at[group(g)], w2.at[group(g), :, mine], ws_sem.at[g], wr_sem.at[g], peer)

    def w_recv(g):
        place = w2.at[group(g), :, others]
        return remote(place, place, ws_sem.at[g], wr_sem.at[g], peer)

    for g in range(groups):
        w_copy(g).start()
        hid_copy(g).start()

    all_experts = nx * experts
    eidx = lax.broadcasted_iota(jnp.int32, (all_experts, toks), 0)
    hot = jnp.zeros((all_experts, toks), F32)
    weight = jnp.zeros((all_experts, toks), F32)
    gf = gates[...].astype(F32)
    rt = routes[...]
    for k in range(top):
        named = rt[k : k + 1, :] == eidx
        hot = jnp.where(named, 1.0, hot)
        weight = jnp.where(named, gf[k : k + 1, :], weight)
    before = lax.broadcasted_iota(jnp.int32, (toks, toks), 0) < lax.broadcasted_iota(
        jnp.int32, (toks, toks), 1
    )
    rank = jnp.dot(hot.astype(BF), before.astype(F32).astype(BF), preferred_element_type=F32)
    rank = jnp.where(hot > 0.5, rank, -1.0)
    for g in range(nx):
        rg_send[g, 0] = rank[g * experts : (g + 1) * experts]
        rg_send[g, 1] = weight[g * experts : (g + 1) * experts]
    rg[x] = rg_send[x]

    pl.semaphore_wait(barrier, len(partners))

    def gox_send(dx):
        return remote(
            go_in, go_all.at[x, :, mine], gox_s.at[dx], gox_r.at[dx], dev(xat(dx), y, c, z)
        )

    def gox_recv(dx):
        place = go_all.at[xat(nx - dx), :, mine]
        return remote(place, place, gox_s.at[dx], gox_r.at[dx], dev(xat(dx), y, c, z))

    def goc_send(dx):
        src = xat(nx - dx)
        place = go_all.at[src, :, mine]
        return remote(place, place, goc_s.at[dx], goc_r.at[dx], peer)

    def goc_recv(dx):
        place = go_all.at[xat(nx - dx), :, others]
        return remote(place, place, goc_s.at[dx], goc_r.at[dx], peer)

    def rg_copy(dx):
        to = xat(dx)
        return remote(
            rg_send.at[to], rg.at[x], rg_s.at[dx], rg_r.at[dx], dev(to, y, c, z)
        )

    def rg_recv(dx):
        place = rg.at[xat(nx - dx)]
        return remote(place, place, rg_s.at[dx], rg_r.at[dx], dev(xat(dx), y, c, z))

    order = sorted(range(1, nx), key=lambda dx: -min(dx, nx - dx))
    for dx in order:
        gox_send(dx).start()
    for dx in order:
        rg_copy(dx).start()
    go_local.wait()
    goc_send(0).start()
    for g in range(groups):
        w_send(g).start()
    for dx in reversed(order):
        gox_recv(dx).wait_recv()
        goc_send(dx).start()
    for dx in reversed(order):
        rg_recv(dx).wait_recv()
    goc_recv(0).wait_recv()
    for dx in reversed(order):
        goc_recv(dx).wait_recv()

    def chain(n, g, d):
        even = mod(g, 2) if d == 0 else 1 - mod(g, 2)
        return n // 2 - even if n % 2 == 0 else jnp.int32(n // 2)

    def y_chunk(buf, i, g):
        return buf.at[i, group(g)]

    def y_msg(d, k, g, src):
        to = dev(x, yat(1 if d == 0 else ny - 1), c, z)
        return remote(
            src, ry.at[d, k, group(g)], ys_sem.at[d, k, g], yr_sem.at[d, k, g], to
        )

    def z_msg(d, k, g, src):
        to = dev(x, y, c, zat(1 if d == 0 else nz - 1))
        return remote(
            src, rz.at[d, k, group(g)], zs_sem.at[d, k, g], zr_sem.at[d, k, g], to
        )

    def away(at, n, d, steps):
        return mod(at + steps, n) if d == 0 else mod(at + n - steps, n)

    rings = (
        (ny, y, ty, ry, y_msg),
        (nz, z, tz, rz, z_msg),
    )

    slot_full = lax.broadcasted_iota(jnp.int32, (cap, toks), 0).astype(F32)
    row = lax.broadcasted_iota(jnp.int32, (half, toks), 0)
    slot_half = (div(row, q) * (2 * q) + c * q + mod(row, q)).astype(F32)
    own_row = lax.broadcasted_iota(jnp.int32, (q, toks), 0)
    slot_own = (own_row + (mod(y, yb) * (2 * q) + c * q)).astype(F32)
    own_block = div(y, yb)
    tile = 256 if h % 256 == 0 else 128

    def produce(g, _):
        hid_copy(g).wait()
        w_copy(g).wait()
        w_recv(g).wait_recv()

        def dispatch(j, _):
            for e in range(per):
                rk = rg[j, 0, pl.ds(g * per + e, 1), :]
                gt = rg[j, 1, pl.ds(g * per + e, 1), :]
                mh[e * half : (e + 1) * half, :] = jnp.where(rk == slot_half, 1.0, 0.0).astype(BF)
                mg[e * cap : (e + 1) * cap, :] = jnp.where(rk == slot_full, gt, 0.0).astype(BF)
            rows = jnp.dot(mh[...], go_all[j], preferred_element_type=F32).astype(BF)
            scaled = jnp.dot(mg[...], go_all[j, :, mine], preferred_element_type=F32).astype(BF)
            dyh[:, pl.ds(pl.multiple_of(j * half, half), half), :] = rows.reshape(
                per, half, 2 * width
            )
            sc[:, pl.ds(pl.multiple_of(j * cap, cap), cap), :] = scaled.reshape(per, cap, width)
            return 0

        lax.fori_loop(0, nx, dispatch, 0)

        def expert(e, _):
            ee = g * per + e
            own_rank = rg[own_block, 0, pl.ds(ee, 1), :]
            own_gate = rg[own_block, 1, pl.ds(ee, 1), :]
            picked = jnp.sum(jnp.where(own_rank == slot_own, own_gate, 0.0), axis=1, keepdims=True)
            gcol[ee] = jnp.broadcast_to(picked, (q, 128))
            rows = dyh[e]
            part = jnp.zeros((lanes, 128), F32)
            for s in range(0, h, tile):
                u = lax.dot_general(
                    rows, w2[ee, s : s + tile, :], (((1,), (1,)), ((), ())),
                    preferred_element_type=F32,
                )
                hh = hid[ee, :, c, :, s : s + tile].reshape(lanes, tile).astype(F32)
                prod = u * hh
                for i in range(0, tile, 128):
                    part = part + prod[:, i : i + 128]
                ty[:, ee, :, s : s + tile] = u.astype(BF).reshape(ny, q, tile)
            gall[y, pl.ds(ee, 1), :] = jnp.sum(part.T, axis=0, keepdims=True)
            wpart = lax.dot_general(
                hid[ee].reshape(2 * lanes, h), sc[e], (((0,), (0,)), ((), ())),
                preferred_element_type=F32,
            )
            tz[:, ee] = wpart.astype(BF).reshape(nz, hz, width)
            return 0

        lax.fori_loop(0, per, expert, 0)
        for n, at, term, buf, msg in rings:
            for d in (0, 1):
                length = chain(n, g, d)

                @pl.when(length > 0)
                def _():
                    dest = away(at, n, d, length)
                    msg(d, 0, g, term.at[dest, group(g)]).start()

        return 0

    lax.fori_loop(0, groups, produce, 0)

    def ga_send(dy):
        return remote(
            gall.at[y], gall.at[y], ga_s.at[dy], ga_r.at[dy], dev(x, yat(dy), c, z)
        )

    def ga_recv(dy):
        place = gall.at[yat(ny - dy)]
        return remote(place, place, ga_s.at[dy], ga_r.at[dy], dev(x, yat(dy), c, z))

    for dy in range(1, ny):
        ga_send(dy).start()

    offsets = [(dx, r) for dx in range(nx) for r in (0, 1) if dx or r]

    def sg_send(dx, r):
        return remote(
            sgx.at[x, c], sgx.at[x, c], sg_s.at[dx, r], sg_r.at[dx, r],
            dev(xat(dx), y, mod(c + r, 2), z),
        )

    def sg_recv(dx, r):
        place = sgx.at[xat(nx - dx), mod(c + r, 2)]
        return remote(
            place, place, sg_s.at[dx, r], sg_r.at[dx, r], dev(xat(dx), y, mod(c + r, 2), z)
        )

    def sum_gates():
        for dy in range(1, ny):
            ga_recv(dy).wait_recv()
        total = gall[0]
        for i in range(1, ny):
            total = total + gall[i]
        sgx[x, c] = total
        for dx, r in offsets:
            sg_send(dx, r).start()

    def place_gates():
        for dx, r in offsets:
            sg_recv(dx, r).wait_recv()
        for g in range(nx):
            slot = jnp.maximum(rg_send[g, 0], 0.0).astype(jnp.int32)
            lane = (x * yb + div(slot, 2 * q)) * q + mod(slot, q)
            odd = mod(div(slot, q), 2) == 1
            for s in range(0, toks, lanes):
                idx = lane[:, s : s + lanes]
                low = jnp.take_along_axis(sgx[g, 0], idx, axis=1, mode="promise_in_bounds")
                high = jnp.take_along_axis(sgx[g, 1], idx, axis=1, mode="promise_in_bounds")
                gsc[g * experts : (g + 1) * experts, s : s + lanes] = jnp.where(
                    odd[:, s : s + lanes], high, low
                )
        chosen = routes[...]
        out = jnp.zeros((top, toks), F32)
        for e in range(all_experts):
            out = jnp.where(chosen == e, gsc[e : e + 1, :], out)
        gg_out[...] = out

    def add_on(n, at, term, buf, msg, unit):
        k = div(unit, groups) + 1
        g = mod(unit, groups)
        last = n // 2
        for d in (0, 1):
            length = chain(n, g, d)

            @pl.when(k < length)
            def _():
                place = buf.at[d, k - 1, group(g)]
                msg(d, k - 1, g, place).wait_recv()
                dest = away(at, n, d, length - k)
                held = buf[d, k - 1, group(g)].astype(F32) + term[dest, group(g)].astype(F32)
                buf[d, k - 1, group(g)] = held.astype(BF)
                msg(d, k, g, place).start()

        return k == last, g

    def finish(n, at, term, buf, msg, g, store):
        for d in (0, 1):
            length = chain(n, g, d)

            @pl.when(length > 0)
            def _():
                msg(d, length - 1, g, buf.at[d, length - 1, group(g)]).wait_recv()

        total = term[at, group(g)].astype(F32)
        for d in (0, 1):
            length = chain(n, g, d)
            came = buf[d, jnp.maximum(length - 1, 0), group(g)].astype(F32)
            if n == 2:
                came = jnp.where(length > 0, came, 0.0)
            total = total + came
        store(total, g)

    def store_y(total, g):
        scale = gcol[group(g)]
        for s in range(0, h, 128):
            gh_out[group(g), :, s : s + 128] = (total[:, :, s : s + 128] * scale).astype(BF)

    def store_z(total, g):
        gw_out[group(g)] = total.astype(BF)

    yu, zu = (ny // 2) * groups, (nz // 2) * groups
    steps = math.gcd(yu, zu)

    def ring_step(s, _):
        for ring, units, store in ((rings[0], yu, store_y), (rings[1], zu, store_z)):
            for i in range(units // steps):
                final, g = add_on(*ring, s * (units // steps) + i)

                @pl.when(final)
                def _():
                    finish(*ring, g, store)

        pl.when(s == steps // 4)(sum_gates)
        pl.when(s == steps // 2)(place_gates)
        return 0

    lax.fori_loop(0, steps, ring_step, 0)

    def drain(g, _):
        w_send(g).wait_send()
        for n, at, term, buf, msg in rings:
            for d in (0, 1):
                length = chain(n, g, d)
                for k in range(n // 2):

                    @pl.when(k < length)
                    def _():
                        msg(d, k, g, term.at[0, group(g)]).wait_send()

        return 0

    lax.fori_loop(0, groups, drain, 0)
    goc_send(0).wait_send()
    for dx in range(1, nx):
        gox_send(dx).wait_send()
        goc_send(dx).wait_send()
        rg_copy(dx).wait_send()
    for dy in range(1, ny):
        ga_send(dy).wait_send()
    for dx, r in offsets:
        sg_send(dx, r).wait_send()


def on_device(nx, ny, nz, groups, grad_out, routes, gates, hidden, w_down):
    experts, slots, h = hidden.shape
    _, toks, width = grad_out.shape
    top = routes.shape[2]
    q = slots // (2 * ny)
    hz = h // nz
    per = experts // groups
    cap = slots // nx
    half = cap // 2
    ky, kz = max(ny // 2, 1), max(nz // 2, 1)
    dma = pltpu.SemaphoreType.DMA
    vmem = pl.BlockSpec(memory_space=pltpu.VMEM)
    anywhere = pl.BlockSpec(memory_space=pl.ANY)
    gh, gw, gg = pl.pallas_call(
        functools.partial(kernel, nx, ny, nz, groups),
        out_shape=(
            jax.ShapeDtypeStruct((experts, q, h), BF),
            jax.ShapeDtypeStruct((experts, hz, width), BF),
            jax.ShapeDtypeStruct((top, toks), F32),
        ),
        in_specs=[anywhere, vmem, vmem, anywhere, anywhere],
        out_specs=(vmem, vmem, vmem),
        scratch_shapes=[
            pltpu.VMEM((experts, ny, 2, q, h), BF),
            pltpu.VMEM((experts, h, 2 * width), BF),
            pltpu.VMEM((nx, toks, 2 * width), BF),
            pltpu.VMEM((nx, 2, experts, toks), F32),
            pltpu.VMEM((nx, 2, experts, toks), F32),
            pltpu.VMEM((per, ny * q, 2 * width), BF),
            pltpu.VMEM((per, slots, width), BF),
            pltpu.VMEM((per * half, toks), BF),
            pltpu.VMEM((per * cap, toks), BF),
            pltpu.VMEM((experts, q, 128), F32),
            pltpu.VMEM((ny, experts, q, h), BF),
            pltpu.VMEM((nz, experts, hz, width), BF),
            pltpu.VMEM((2, ky, experts, q, h), BF),
            pltpu.VMEM((2, kz, experts, hz, width), BF),
            pltpu.VMEM((ny, experts, ny * q), F32),
            pltpu.VMEM((nx, 2, experts, ny * q), F32),
            pltpu.VMEM((nx * experts, toks), F32),
            dma((groups,)),
            dma((groups,)),
            dma((groups,)),
            dma((groups,)),
            dma,
            dma((nx,)),
            dma((nx,)),
            dma((nx,)),
            dma((nx,)),
            dma((nx,)),
            dma((nx,)),
            dma((2, ky, groups)),
            dma((2, ky, groups)),
            dma((2, kz, groups)),
            dma((2, kz, groups)),
            dma((ny,)),
            dma((ny,)),
            dma((nx, 2)),
            dma((nx, 2)),
        ],
        compiler_params=pltpu.CompilerParams(
            collective_id=0, has_side_effects=True, vmem_limit_bytes=58 * 1024 * 1024
        ),
    )(
        grad_out.reshape(toks, width),
        routes.reshape(toks, top).T,
        gates.reshape(toks, top).T,
        hidden.reshape(experts, ny, 2, q, h),
        w_down,
    )
    return gh, gw, gg.T.reshape(1, toks, top)


def solution(mesh):
    nx, ny, nz = mesh.shape["expert"], mesh.shape["tensor"] // 2, mesh.shape["dp"]
    groups = 4
    placed = (
        P("dp", "expert", "tensor"),
        P("dp", "expert", None),
        P("dp", "expert", None),
        P("expert", "dp", None),
        P("expert", None, "tensor"),
    )
    return jax.shard_map(
        functools.partial(on_device, nx, ny, nz, groups),
        mesh=mesh,
        in_specs=placed,
        out_specs=(
            P("expert", ("dp", "tensor"), None),
            P("expert", "dp", "tensor"),
            P("dp", "expert", None),
        ),
        check_vma=False,
    )
```

time: 279 us -> 76 us (0.27); the launches traced: 275 us -> 75.7 us
  Pallas kernels: 0 us -> 70.3 us
  waiting for transfers between devices: 67.8 us -> 0 us
  local copies, waits for them, and re-layouts: 67.4 us -> 4.73 us
  blocking collectives: 54.6 us -> 0 us
  other arithmetic: 40.1 us -> 0 us
  matrix products: 17.8 us -> 0 us
  between operations: 14.2 us -> 0.64 us
  starting transfers between devices: 12.6 us -> 0 us
    pallas_call x0 -> x1, Pallas kernels: none -> 70.3 us  [on_device(): pl.pallas_call(functools.partial(kernel, nx, ny, nz, groups), out_shape=(...]
    psum x1 -> x0, blocking collectives: 54.6 us -> none  [on_device(): gate_total = lax.psum(gate_part, 'tensor')]
    reduce_scatter x2 -> x0, waiting for transfers between devices: 54.2 us -> none  [the longest x1 54.2 us: on_device(): lax.psum_scatter(hidden_term.astype(jnp.bfloat16), 'tensor', scatter_dime...]
    another operation x3 -> x0, other arithmetic: 36 us -> none
    scatter x2 -> x0, local copies, waits for them, and re-layouts: 35.3 us -> none  [the longest x1 20.7 us: on_device(): jnp.zeros((experts * capacity, width_part), jnp.bfloat16).at[target]]
    dot_general x3 -> x0, matrix products: 17.8 us -> none  [the longest x1 6.1 us: on_device(): jnp.einsum('esd,ehd->esh', scaled, w_down, preferred_element_type=jnp.flo...]
    all_to_all x3 -> x0, waiting for transfers between devices: 13.6 us -> none  [the longest x1 9.41 us: on_device(): lax.all_to_all(sent_rows.reshape(groups, local_experts, capacity, width_p...]
    all_to_all x3 -> x0, starting transfers between devices: 12.3 us -> none  [the longest x1 4.84 us: on_device(): lax.all_to_all(sent_gates.reshape(groups, local_experts, capacity), 'expe...]
  transfers between devices with their start and end apart: 5 -> 0, of which waited for: 3 -> 0; matrix products, arithmetic and copies ran while one was open for 19% -> 0% of each run, Pallas kernels for 0% -> 0%
where the time goes in v1:
time: 76 us; the launch traced here: 75.7 us
  Pallas kernels  70.3 us (92%)
  local copies, waits for them, and re-layouts  4.73 us (6%)
    pallas_call x1, Pallas kernels, on_device(): pl.pallas_call(functools.partial(kernel, nx, ny, nz, groups), out_shape=(...  70.3 us
    unnamed x3, local copies, waits for them, and re-layouts  4.73 us

profile of v1, /device:TPU:1, one launch (start us, length us, event | category | flops | bytes accessed | tf_op | source)
XLA Modules:
  0.0 75.7 jit_solution(5799621724851414622)
XLA Ops:
  0.6 70.3 %shard_map.76 = (bf16[16,16,768]{2,1,0:T(8,128)(2,1)}, bf16[16,64,128]{2,1,0:T(8,128)(2,1)}, f32[8,256]{1,0:T(8,128)}) custom-call(bf16[256,128]{1,0:T(8,128)(2,1)} %bitcast.12, s32[8,256]{1,0:T(8,128)} %bitcast.13, bf16[8,256]{1,0:T(8,128)(2,1)} %bitcast.15, bf16[16,8,2,16,768]{4,3,2,1,0:T(8,128)(2,1)} %bitcast.11, bf16[16,768,128]{2,1,0:T(8,128)(2,1)} %w_in.1), custom_call_target="tpu_custom_call" | custom-call | tf_op jit(solution)/shard_map/pallas_call | solution.py:422
  71.0 1.8 %copy.11 = bf16[16,16,768]{2,1,0:T(8,128)(2,1)} copy(bf16[16,16,768]{2,1,0:T(8,128)(2,1)} %get-tuple-element.12) | data formatting | bytes 786432
  72.7 1.7 %copy.12 = bf16[16,64,128]{2,1,0:T(8,128)(2,1)} copy(bf16[16,64,128]{2,1,0:T(8,128)(2,1)} %get-tuple-element.13) | data formatting | bytes 524288
  74.4 1.3 %copy.13 = f32[1,256,8]{1,2,0:T(8,128)} copy(f32[1,256,8]{1,2,0:T(8,128)} %bitcast.14) | data formatting | bytes 16384

commit v2 on v1

--- a/solution.py
+++ b/solution.py
@@ -1,5 +1,5 @@
 import functools
-import math
+import heapq
 
 import jax
 import jax.numpy as jnp
@@ -21,12 +21,48 @@
     return lax.div(a, jnp.int32(n))
 
 
+def timeline(ny, nz, groups):
+    size = {0: 8.8 / groups, 1: 5.8 / groups}
+    steps = {0: ny // 2, 1: nz // 2}
+    work = {"make": 5.4 / groups, "add": 1.6 / groups}
+    latency = 1.8
+    makes = [(r, g) for g in range(groups) for r in (1, 0)]
+    free = {0: 0.0, 1: 0.0}
+    ready, order, now, gate = [], [], 0.0, None
+
+    def send(r, k, g, at):
+        free[r] = max(free[r], at) + size[r]
+        heapq.heappush(ready, (free[r] + latency, r, k + 1, g))
+
+    while makes or ready or gate:
+        if gate and gate[0] <= now:
+            order.append(("gate", 0, gate[1], 0))
+            now += 0.3
+            gate = (now + 6.0, gate[1] + 1) if gate[1] < 2 else None
+        elif ready and (ready[0][0] <= now or not makes):
+            arrived, r, k, g = heapq.heappop(ready)
+            now = max(now, arrived) + work["add"]
+            order.append(("end" if k == steps[r] else "add", r, k, g))
+            if k < steps[r]:
+                send(r, k, g, now)
+        elif makes:
+            r, g = makes.pop(0)
+            now += work["make"]
+            order.append(("make", r, 0, g))
+            send(r, 0, g, now)
+            if not makes:
+                gate = (now, 0)
+        else:
+            now = gate[0]
+    return order
+
+
 def kernel(
     nx, ny, nz, groups,
     go_in, routes, gates, hid_in, w_in,
     gh_out, gw_out, gg_out,
     hid, w2, go_all, rg_send, rg, dyh, sc, mh, mg, gcol,
-    ty, tz, ry, rz, gall, sgx, gsc,
+    ty, tz, ry, rz, gall, sgx, gsc, rgf,
     hid_sem, wl_sem, ws_sem, wr_sem, go_l, gox_s, gox_r, goc_s, goc_r, rg_s, rg_r,
     ys_sem, yr_sem, zs_sem, zr_sem, ga_s, ga_r, sg_s, sg_r,
 ):
@@ -100,6 +136,44 @@
         w_copy(g).start()
         hid_copy(g).start()
 
+    pl.semaphore_wait(barrier, len(partners))
+
+    def gox_send(dx):
+        return remote(
+            go_in, go_all.at[x, :, mine], gox_s.at[dx], gox_r.at[dx], dev(xat(dx), y, c, z)
+        )
+
+    def gox_recv(dx):
+        place = go_all.at[xat(nx - dx), :, mine]
+        return remote(place, place, gox_s.at[dx], gox_r.at[dx], dev(xat(dx), y, c, z))
+
+    def goc_send(dx):
+        src = xat(nx - dx)
+        place = go_all.at[src, :, mine]
+        return remote(place, place, goc_s.at[dx], goc_r.at[dx], peer)
+
+    def goc_recv(dx):
+        place = go_all.at[xat(nx - dx), :, others]
+        return remote(place, place, goc_s.at[dx], goc_r.at[dx], peer)
+
+    def rg_copy(dx):
+        to = xat(dx)
+        return remote(
+            rg_send.at[to], rg.at[x], rg_s.at[dx], rg_r.at[dx], dev(to, y, c, z)
+        )
+
+    def rg_recv(dx):
+        place = rg.at[xat(nx - dx)]
+        return remote(place, place, rg_s.at[dx], rg_r.at[dx], dev(xat(dx), y, c, z))
+
+    order = sorted(range(1, nx), key=lambda dx: -min(dx, nx - dx))
+    for dx in order:
+        gox_send(dx).start()
+    go_local.wait()
+    goc_send(0).start()
+    for g in range(groups):
+        w_send(g).start()
+
     all_experts = nx * experts
     eidx = lax.broadcasted_iota(jnp.int32, (all_experts, toks), 0)
     hot = jnp.zeros((all_experts, toks), F32)
@@ -116,64 +190,20 @@
     rank = jnp.dot(hot.astype(BF), before.astype(F32).astype(BF), preferred_element_type=F32)
     rank = jnp.where(hot > 0.5, rank, -1.0)
     for g in range(nx):
-        rg_send[g, 0] = rank[g * experts : (g + 1) * experts]
-        rg_send[g, 1] = weight[g * experts : (g + 1) * experts]
+        rg_send[g, 0] = rank[g * experts : (g + 1) * experts].astype(BF)
+        rg_send[g, 1] = weight[g * experts : (g + 1) * experts].astype(BF)
     rg[x] = rg_send[x]
-
-    pl.semaphore_wait(barrier, len(partners))
-
-    def gox_send(dx):
-        return remote(
-            go_in, go_all.at[x, :, mine], gox_s.at[dx], gox_r.at[dx], dev(xat(dx), y, c, z)
-        )
-
-    def gox_recv(dx):
-        place = go_all.at[xat(nx - dx), :, mine]
-        return remote(place, place, gox_s.at[dx], gox_r.at[dx], dev(xat(dx), y, c, z))
-
-    def goc_send(dx):
-        src = xat(nx - dx)
-        place = go_all.at[src, :, mine]
-        return remote(place, place, goc_s.at[dx], goc_r.at[dx], peer)
-
-    def goc_recv(dx):
-        place = go_all.at[xat(nx - dx), :, others]
-        return remote(place, place, goc_s.at[dx], goc_r.at[dx], peer)
-
-    def rg_copy(dx):
-        to = xat(dx)
-        return remote(
-            rg_send.at[to], rg.at[x], rg_s.at[dx], rg_r.at[dx], dev(to, y, c, z)
-        )
-
-    def rg_recv(dx):
-        place = rg.at[xat(nx - dx)]
-        return remote(place, place, rg_s.at[dx], rg_r.at[dx], dev(xat(dx), y, c, z))
-
-    order = sorted(range(1, nx), key=lambda dx: -min(dx, nx - dx))
-    for dx in order:
-        gox_send(dx).start()
     for dx in order:
         rg_copy(dx).start()
-    go_local.wait()
-    goc_send(0).start()
-    for g in range(groups):
-        w_send(g).start()
     for dx in reversed(order):
         gox_recv(dx).wait_recv()
         goc_send(dx).start()
     for dx in reversed(order):
         rg_recv(dx).wait_recv()
-    goc_recv(0).wait_recv()
-    for dx in reversed(order):
-        goc_recv(dx).wait_recv()
+    rgf[...] = rg[...].astype(F32)
 
     def chain(n, g, d):
-        even = mod(g, 2) if d == 0 else 1 - mod(g, 2)
-        return n // 2 - even if n % 2 == 0 else jnp.int32(n // 2)
-
-    def y_chunk(buf, i, g):
-        return buf.at[i, group(g)]
+        return n // 2 - (g + d) % 2 if n % 2 == 0 else n // 2
 
     def y_msg(d, k, g, src):
         to = dev(x, yat(1 if d == 0 else ny - 1), c, z)
@@ -203,31 +233,61 @@
     own_block = div(y, yb)
     tile = 256 if h % 256 == 0 else 128
 
-    def produce(g, _):
+    def start_ring(ring, g):
+        n, at, term, buf, msg = ring
+        for d in (0, 1):
+            length = chain(n, g, d)
+            if length > 0:
+                dest = away(at, n, d, length)
+                msg(d, 0, g, term.at[dest, group(g)]).start()
+
+    def make_weight(g):
         hid_copy(g).wait()
+
+        def dispatch(j, _):
+            for e in range(per):
+                rk = rgf[j, 0, pl.ds(g * per + e, 1), :]
+                gt = rgf[j, 1, pl.ds(g * per + e, 1), :]
+                mg[e * cap : (e + 1) * cap, :] = jnp.where(rk == slot_full, gt, 0.0).astype(BF)
+            scaled = jnp.dot(mg[...], go_all[j, :, mine], preferred_element_type=F32).astype(BF)
+            sc[:, pl.ds(pl.multiple_of(j * cap, cap), cap), :] = scaled.reshape(per, cap, width)
+            return 0
+
+        def expert(e, _):
+            ee = g * per + e
+            wpart = lax.dot_general(
+                hid[ee].reshape(2 * lanes, h), sc[e], (((0,), (0,)), ((), ())),
+                preferred_element_type=F32,
+            )
+            tz[:, ee] = wpart.astype(BF).reshape(nz, hz, width)
+            return 0
+
+        lax.fori_loop(0, nx, dispatch, 0)
+        lax.fori_loop(0, per, expert, 0)
+        start_ring(rings[1], g)
+
+    def make_hidden(g):
+        if g == 0:
+            goc_recv(0).wait_recv()
+            for dx in reversed(order):
+                goc_recv(dx).wait_recv()
         w_copy(g).wait()
         w_recv(g).wait_recv()
 
         def dispatch(j, _):
             for e in range(per):
-                rk = rg[j, 0, pl.ds(g * per + e, 1), :]
-                gt = rg[j, 1, pl.ds(g * per + e, 1), :]
+                rk = rgf[j, 0, pl.ds(g * per + e, 1), :]
                 mh[e * half : (e + 1) * half, :] = jnp.where(rk == slot_half, 1.0, 0.0).astype(BF)
-                mg[e * cap : (e + 1) * cap, :] = jnp.where(rk == slot_full, gt, 0.0).astype(BF)
             rows = jnp.dot(mh[...], go_all[j], preferred_element_type=F32).astype(BF)
-            scaled = jnp.dot(mg[...], go_all[j, :, mine], preferred_element_type=F32).astype(BF)
             dyh[:, pl.ds(pl.multiple_of(j * half, half), half), :] = rows.reshape(
                 per, half, 2 * width
             )
-            sc[:, pl.ds(pl.multiple_of(j * cap, cap), cap), :] = scaled.reshape(per, cap, width)
             return 0
-
-        lax.fori_loop(0, nx, dispatch, 0)
 
         def expert(e, _):
             ee = g * per + e
-            own_rank = rg[own_block, 0, pl.ds(ee, 1), :]
-            own_gate = rg[own_block, 1, pl.ds(ee, 1), :]
+            own_rank = rgf[own_block, 0, pl.ds(ee, 1), :]
+            own_gate = rgf[own_block, 1, pl.ds(ee, 1), :]
             picked = jnp.sum(jnp.where(own_rank == slot_own, own_gate, 0.0), axis=1, keepdims=True)
             gcol[ee] = jnp.broadcast_to(picked, (q, 128))
             rows = dyh[e]
@@ -243,26 +303,11 @@
                     part = part + prod[:, i : i + 128]
                 ty[:, ee, :, s : s + tile] = u.astype(BF).reshape(ny, q, tile)
             gall[y, pl.ds(ee, 1), :] = jnp.sum(part.T, axis=0, keepdims=True)
-            wpart = lax.dot_general(
-                hid[ee].reshape(2 * lanes, h), sc[e], (((0,), (0,)), ((), ())),
-                preferred_element_type=F32,
-            )
-            tz[:, ee] = wpart.astype(BF).reshape(nz, hz, width)
             return 0
 
+        lax.fori_loop(0, nx, dispatch, 0)
         lax.fori_loop(0, per, expert, 0)
-        for n, at, term, buf, msg in rings:
-            for d in (0, 1):
-                length = chain(n, g, d)
-
-                @pl.when(length > 0)
-                def _():
-                    dest = away(at, n, d, length)
-                    msg(d, 0, g, term.at[dest, group(g)]).start()
-
-        return 0
-
-    lax.fori_loop(0, groups, produce, 0)
+        start_ring(rings[0], g)
 
     def ga_send(dy):
         return remote(
@@ -273,8 +318,9 @@
         place = gall.at[yat(ny - dy)]
         return remote(place, place, ga_s.at[dy], ga_r.at[dy], dev(x, yat(dy), c, z))
 
-    for dy in range(1, ny):
-        ga_send(dy).start()
+    def send_gates():
+        for dy in range(1, ny):
+            ga_send(dy).start()
 
     offsets = [(dx, r) for dx in range(nx) for r in (0, 1) if dx or r]
 
@@ -304,7 +350,7 @@
         for dx, r in offsets:
             sg_recv(dx, r).wait_recv()
         for g in range(nx):
-            slot = jnp.maximum(rg_send[g, 0], 0.0).astype(jnp.int32)
+            slot = jnp.maximum(rg_send[g, 0].astype(F32), 0.0).astype(jnp.int32)
             lane = (x * yb + div(slot, 2 * q)) * q + mod(slot, q)
             odd = mod(div(slot, q), 2) == 1
             for s in range(0, toks, lanes):
@@ -320,81 +366,66 @@
             out = jnp.where(chosen == e, gsc[e : e + 1, :], out)
         gg_out[...] = out
 
-    def add_on(n, at, term, buf, msg, unit):
-        k = div(unit, groups) + 1
-        g = mod(unit, groups)
-        last = n // 2
+    def add_on(ring, k, g):
+        n, at, term, buf, msg = ring
         for d in (0, 1):
             length = chain(n, g, d)
-
-            @pl.when(k < length)
-            def _():
+            if k < length:
                 place = buf.at[d, k - 1, group(g)]
                 msg(d, k - 1, g, place).wait_recv()
                 dest = away(at, n, d, length - k)
-                held = buf[d, k - 1, group(g)].astype(F32) + term[dest, group(g)].astype(F32)
-                buf[d, k - 1, group(g)] = held.astype(BF)
+
+                def one(e, _):
+                    ee = g * per + e
+                    held = buf[d, k - 1, ee].astype(F32) + term[dest, ee].astype(F32)
+                    buf[d, k - 1, ee] = held.astype(BF)
+                    return 0
+
+                lax.fori_loop(0, per, one, 0)
                 msg(d, k, g, place).start()
 
-        return k == last, g
-
-    def finish(n, at, term, buf, msg, g, store):
+    def finish(ring, g, store):
+        n, at, term, buf, msg = ring
+        lengths = [chain(n, g, d) for d in (0, 1)]
         for d in (0, 1):
-            length = chain(n, g, d)
-
-            @pl.when(length > 0)
-            def _():
-                msg(d, length - 1, g, buf.at[d, length - 1, group(g)]).wait_recv()
-
-        total = term[at, group(g)].astype(F32)
-        for d in (0, 1):
-            length = chain(n, g, d)
-            came = buf[d, jnp.maximum(length - 1, 0), group(g)].astype(F32)
-            if n == 2:
-                came = jnp.where(length > 0, came, 0.0)
-            total = total + came
-        store(total, g)
+            if lengths[d] > 0:
+                msg(d, lengths[d] - 1, g, buf.at[d, lengths[d] - 1, group(g)]).wait_recv()
+
+        def one(e, _):
+            ee = g * per + e
+            total = term[at, ee].astype(F32)
+            for d in (0, 1):
+                if lengths[d] > 0:
+                    total = total + buf[d, lengths[d] - 1, ee].astype(F32)
+            store(total, ee)
+            return 0
+
+        lax.fori_loop(0, per, one, 0)
 
     def store_y(total, g):
-        scale = gcol[group(g)]
+        scale = gcol[g]
         for s in range(0, h, 128):
-            gh_out[group(g), :, s : s + 128] = (total[:, :, s : s + 128] * scale).astype(BF)
+            gh_out[g, :, s : s + 128] = (total[:, s : s + 128] * scale).astype(BF)
 
     def store_z(total, g):
-        gw_out[group(g)] = total.astype(BF)
-
-    yu, zu = (ny // 2) * groups, (nz // 2) * groups
-    steps = math.gcd(yu, zu)
-
-    def ring_step(s, _):
-        for ring, units, store in ((rings[0], yu, store_y), (rings[1], zu, store_z)):
-            for i in range(units // steps):
-                final, g = add_on(*ring, s * (units // steps) + i)
-
-                @pl.when(final)
-                def _():
-                    finish(*ring, g, store)
-
-        pl.when(s == steps // 4)(sum_gates)
-        pl.when(s == steps // 2)(place_gates)
-        return 0
-
-    lax.fori_loop(0, steps, ring_step, 0)
-
-    def drain(g, _):
+        gw_out[g] = total.astype(BF)
+
+    for what, ring, k, g in timeline(ny, nz, groups):
+        if what == "make":
+            (make_hidden, make_weight)[ring](g)
+        elif what == "add":
+            add_on(rings[ring], k, g)
+        elif what == "end":
+            finish(rings[ring], g, (store_y, store_z)[ring])
+        else:
+            (send_gates, sum_gates, place_gates)[k]()
+
+    for g in range(groups):
         w_send(g).wait_send()
         for n, at, term, buf, msg in rings:
             for d in (0, 1):
-                length = chain(n, g, d)
-                for k in range(n // 2):
-
-                    @pl.when(k < length)
-                    def _():
-                        msg(d, k, g, term.at[0, group(g)]).wait_send()
-
-        return 0
-
-    lax.fori_loop(0, groups, drain, 0)
+                for k in range(chain(n, g, d)):
+                    msg(d, k, g, term.at[0, group(g)]).wait_send()
     goc_send(0).wait_send()
     for dx in range(1, nx):
         gox_send(dx).wait_send()
@@ -432,8 +463,8 @@
             pltpu.VMEM((experts, ny, 2, q, h), BF),
             pltpu.VMEM((experts, h, 2 * width), BF),
             pltpu.VMEM((nx, toks, 2 * width), BF),
-            pltpu.VMEM((nx, 2, experts, toks), F32),
-            pltpu.VMEM((nx, 2, experts, toks), F32),
+            pltpu.VMEM((nx, 2, experts, toks), BF),
+            pltpu.VMEM((nx, 2, experts, toks), BF),
             pltpu.VMEM((per, ny * q, 2 * width), BF),
             pltpu.VMEM((per, slots, width), BF),
             pltpu.VMEM((per * half, toks), BF),
@@ -446,6 +477,7 @@
             pltpu.VMEM((ny, experts, ny * q), F32),
             pltpu.VMEM((nx, 2, experts, ny * q), F32),
             pltpu.VMEM((nx * experts, toks), F32),
+            pltpu.VMEM((nx, 2, experts, toks), F32),
             dma((groups,)),
             dma((groups,)),
             dma((groups,)),

time: 76 us -> 74.2 us (0.976); the launches traced: 75.7 us -> 73 us
  Pallas kernels: 70.3 us -> 67.7 us
    pallas_call x1, Pallas kernels: 70.3 us -> 67.7 us  [on_device(): pl.pallas_call(functools.partial(kernel, nx, ny, nz, groups), out_shape=(...]
where the time goes in v2:
time: 74.2 us; the launch traced here: 73 us
  Pallas kernels  67.7 us (91%)
  local copies, waits for them, and re-layouts  4.73 us (6%)
    pallas_call x1, Pallas kernels, on_device(): pl.pallas_call(functools.partial(kernel, nx, ny, nz, groups), out_shape=(...  67.7 us
    unnamed x3, local copies, waits for them, and re-layouts  4.73 us

profile of v2, /device:TPU:1, one launch (start us, length us, event | category | flops | bytes accessed | tf_op | source)
XLA Modules:
  0.0 73.0 jit_solution(5747041883605216232)
XLA Ops:
  0.6 67.7 %shard_map.76 = (bf16[16,16,768]{2,1,0:T(8,128)(2,1)}, bf16[16,64,128]{2,1,0:T(8,128)(2,1)}, f32[8,256]{1,0:T(8,128)}) custom-call(bf16[256,128]{1,0:T(8,128)(2,1)} %bitcast.12, s32[8,256]{1,0:T(8,128)} %bitcast.13, bf16[8,256]{1,0:T(8,128)(2,1)} %bitcast.15, bf16[16,8,2,16,768]{4,3,2,1,0:T(8,128)(2,1)} %bitcast.11, bf16[16,768,128]{2,1,0:T(8,128)(2,1)} %w_in.1), custom_call_target="tpu_custom_call" | custom-call | tf_op jit(solution)/shard_map/pallas_call | solution.py:453
  68.3 1.8 %copy.11 = bf16[16,16,768]{2,1,0:T(8,128)(2,1)} copy(bf16[16,16,768]{2,1,0:T(8,128)(2,1)} %get-tuple-element.12) | data formatting | bytes 786432
  70.1 1.7 %copy.12 = bf16[16,64,128]{2,1,0:T(8,128)(2,1)} copy(bf16[16,64,128]{2,1,0:T(8,128)(2,1)} %get-tuple-element.13) | data formatting | bytes 524288
  71.7 1.3 %copy.13 = f32[1,256,8]{1,2,0:T(8,128)} copy(f32[1,256,8]{1,2,0:T(8,128)} %bitcast.14) | data formatting | bytes 16384

commit v3 on v2

--- a/solution.py
+++ b/solution.py
@@ -365,6 +365,21 @@
         for e in range(all_experts):
             out = jnp.where(chosen == e, gsc[e : e + 1, :], out)
         gg_out[...] = out
+        for g in range(groups):
+            w_send(g).wait_send()
+        goc_send(0).wait_send()
+        for dx in range(1, nx):
+            gox_send(dx).wait_send()
+            goc_send(dx).wait_send()
+            rg_copy(dx).wait_send()
+        for dy in range(1, ny):
+            ga_send(dy).wait_send()
+
+    def left(ring, k, g):
+        n, at, term, buf, msg = ring
+        for d in (0, 1):
+            if k - 1 < chain(n, g, d):
+                msg(d, k - 1, g, term.at[0, group(g)]).wait_send()
 
     def add_on(ring, k, g):
         n, at, term, buf, msg = ring
@@ -383,6 +398,7 @@
 
                 lax.fori_loop(0, per, one, 0)
                 msg(d, k, g, place).start()
+        left(ring, k, g)
 
     def finish(ring, g, store):
         n, at, term, buf, msg = ring
@@ -401,6 +417,7 @@
             return 0
 
         lax.fori_loop(0, per, one, 0)
+        left(ring, n // 2, g)
 
     def store_y(total, g):
         scale = gcol[g]
@@ -420,19 +437,6 @@
         else:
             (send_gates, sum_gates, place_gates)[k]()
 
-    for g in range(groups):
-        w_send(g).wait_send()
-        for n, at, term, buf, msg in rings:
-            for d in (0, 1):
-                for k in range(chain(n, g, d)):
-                    msg(d, k, g, term.at[0, group(g)]).wait_send()
-    goc_send(0).wait_send()
-    for dx in range(1, nx):
-        gox_send(dx).wait_send()
-        goc_send(dx).wait_send()
-        rg_copy(dx).wait_send()
-    for dy in range(1, ny):
-        ga_send(dy).wait_send()
     for dx, r in offsets:
         sg_send(dx, r).wait_send()
 

time: 74.2 us -> 74.1 us (level)
  no operation moved by 1% of the time
where the time goes in v3:
time: 74.1 us; the launch traced here: 72.9 us
  Pallas kernels  67.5 us (91%)
  local copies, waits for them, and re-layouts  4.73 us (6%)
    pallas_call x1, Pallas kernels, on_device(): pl.pallas_call(functools.partial(kernel, nx, ny, nz, groups), out_shape=(...  67.5 us
    unnamed x3, local copies, waits for them, and re-layouts  4.73 us

profile of v3, /device:TPU:1, one launch (start us, length us, event | category | flops | bytes accessed | tf_op | source)
XLA Modules:
  0.0 72.9 jit_solution(8492673990020195014)
XLA Ops:
  0.6 67.5 %shard_map.76 = (bf16[16,16,768]{2,1,0:T(8,128)(2,1)}, bf16[16,64,128]{2,1,0:T(8,128)(2,1)}, f32[8,256]{1,0:T(8,128)}) custom-call(bf16[256,128]{1,0:T(8,128)(2,1)} %bitcast.12, s32[8,256]{1,0:T(8,128)} %bitcast.13, bf16[8,256]{1,0:T(8,128)(2,1)} %bitcast.15, bf16[16,8,2,16,768]{4,3,2,1,0:T(8,128)(2,1)} %bitcast.11, bf16[16,768,128]{2,1,0:T(8,128)(2,1)} %w_in.1), custom_call_target="tpu_custom_call" | custom-call | tf_op jit(solution)/shard_map/pallas_call | solution.py:457
  68.2 1.8 %copy.11 = bf16[16,16,768]{2,1,0:T(8,128)(2,1)} copy(bf16[16,16,768]{2,1,0:T(8,128)(2,1)} %get-tuple-element.12) | data formatting | bytes 786432
  69.9 1.7 %copy.12 = bf16[16,64,128]{2,1,0:T(8,128)(2,1)} copy(bf16[16,64,128]{2,1,0:T(8,128)(2,1)} %get-tuple-element.13) | data formatting | bytes 524288
  71.6 1.3 %copy.13 = f32[1,256,8]{1,2,0:T(8,128)} copy(f32[1,256,8]{1,2,0:T(8,128)} %bitcast.14) | data formatting | bytes 16384
